TPU v7x, 32 devices: a whole 2x2x4 slice. The times are simulated.
32 devices in a mesh: dp: 16 (over z, y, x), tensor: 2 (over core).
Axes of the slice: x: 2, y: 2, z: 4, core: 2. Of those that a mesh axis runs over, the one named last changes fastest.
Arguments:
- tokens: bfloat16 [8192, 1024], P(('dp', 'tensor')), may hold values from -12 to 12
- enc_states: bfloat16 [4096, 1024], P(('dp', 'tensor')), may hold values from -12 to 12
- utt_lengths: int32 [16], P('dp'), may hold values from 256 to 512, as said below
- enc_lengths: int32 [16], P('dp'), may hold values from 128 to 256, as said below
- self_qkv: bfloat16 [3, 1024, 1024], P(None, 'dp', 'tensor'), may hold values from -0.1875 to 0.1875
- self_out: bfloat16 [1024, 1024], P('dp', 'tensor'), may hold values from -2 to 2
- cross_qkv: bfloat16 [3, 1024, 1024], P(None, 'dp', 'tensor'), may hold values from -0.1875 to 0.1875
- cross_out: bfloat16 [1024, 1024], P('dp', 'tensor'), may hold values from -1.5 to 1.5
- ffn_proj: bfloat16 [2, 1024, 4096], P(None, 'dp', 'tensor'), may hold values from -0.1875 to 0.1875
- norm_gains: bfloat16 [4, 1024], P(None, 'dp'), may hold values from 0.25 to 1.75
- norm_biases: bfloat16 [4, 1024], P(None, 'dp'), may hold values from -1.25 to 1.25
- cotangent: bfloat16 [8192, 1024], P(('dp', 'tensor')), may hold values from -12 to 12
Outputs:
- output: bfloat16 [8192, 1024], P(('dp', 'tensor'))
- token_grad: float32 [8192, 1024], P(('dp', 'tensor'))
- enc_grad: float32 [4096, 1024], P(('dp', 'tensor'))
- self_qkv_grad: float32 [3, 1024, 1024], P(None, 'dp', 'tensor')
- self_out_grad: float32 [1024, 1024], P('dp', 'tensor')
- cross_qkv_grad: float32 [3, 1024, 1024], P(None, 'dp', 'tensor')
- cross_out_grad: float32 [1024, 1024], P('dp', 'tensor')
- ffn_grad: float32 [2, 1024, 4096], P(None, 'dp', 'tensor')
- gains_grad: float32 [4, 1024], P(None, ('dp', 'tensor'))
- biases_grad: float32 [4, 1024], P(None, ('dp', 'tensor'))
Inputs may be any that keep to these rules, and one draw needn't show every extreme that they name: `utt_lengths`: valid unit tokens of each utterance; at least one utterance fills all 512 slots. `enc_lengths`: valid encoder states of each utterance; at least one utterance fills all 256 slots.
All inputs are finite; a program needn't handle non-finite values.
Results may differ from a plain program's by a relative error of at most 0.035.
Values may be sent and summed in bfloat16 or wider, within the bound.
No kernel may reach another device: no remote copies, remote signals or barrier semaphores. Data moves between devices by JAX's collectives and lax.ppermute only.
A program may use at most 192 MiB of HBM per device.

v0:
```python
import jax
import jax.numpy as jnp
from jax import lax
from jax.sharding import PartitionSpec as P

HEAD_DIM = 64


EPSILON = 1e-05
NEG_FILL = -1000000000.0


def layer_norm(values, gain, shift):
    centre = jnp.mean(values, axis=-1, keepdims=True)
    centred = values - centre
    spread = jnp.mean(centred * centred, axis=-1, keepdims=True)
    return centred * lax.rsqrt(spread + EPSILON) * gain + shift


def gelu_tanh(values):
    return jax.nn.gelu(values, approximate=True)


def norm_back(values, gain, shift, grad):
    unused, pullback = jax.vjp(layer_norm, values, gain, shift)
    return pullback(grad)


def gather_rows(values):
    return lax.all_gather(values, "tensor", axis=0, tiled=True)


def gather_grads(values):
    return lax.all_gather(values, "tensor", axis=0, tiled=True)


def sum_branch(values):
    return lax.psum_scatter(
        values.astype(jnp.bfloat16), "tensor", scatter_dimension=0, tiled=True
    ).astype(jnp.float32)


def sum_inputs(values):
    return lax.psum_scatter(
        values.astype(jnp.bfloat16), "tensor", scatter_dimension=0, tiled=True
    ).astype(jnp.float32)


def block_scores(query_block, key_heads, allowed, scale):
    raw = (
        jnp.einsum("qhd,khd->hqk", query_block, key_heads, preferred_element_type=jnp.float32)
        * scale
    )
    return jnp.where(allowed[None], raw, NEG_FILL)


def attention_forward(queries, keys, values, allowed_at, block):
    rows, cols = queries.shape
    heads = cols // HEAD_DIM
    count = keys.shape[0]
    scale = HEAD_DIM ** (-0.5)
    query_blocks = queries.reshape(rows // block, block, heads, HEAD_DIM)
    starts = jnp.arange(rows // block, dtype=jnp.int32) * block
    key_heads = keys.reshape(count, heads, HEAD_DIM)
    value_heads = values.reshape(count, heads, HEAD_DIM)

    def one_block(item):
        query_block, start = item
        scores = block_scores(query_block, key_heads, allowed_at(start, block), scale)
        top = jnp.max(scores, axis=-1, keepdims=True)
        exps = jnp.exp(scores - top)
        total = jnp.sum(exps, axis=-1, keepdims=True)
        weights = (exps / total).astype(jnp.bfloat16)
        mixed = jnp.einsum("hqk,khd->qhd", weights, value_heads, preferred_element_type=jnp.float32)
        return (mixed.astype(jnp.bfloat16).reshape(block, cols), (top + jnp.log(total))[..., 0])

    mixed, log_totals = lax.map(one_block, (query_blocks, starts))
    return (mixed.reshape(rows, cols), log_totals)


def attention_backward(queries, keys, values, grad_mixed, log_totals, allowed_at, block):
    rows, cols = queries.shape
    heads = cols // HEAD_DIM
    count = keys.shape[0]
    scale = HEAD_DIM ** (-0.5)
    query_blocks = queries.reshape(rows // block, block, heads, HEAD_DIM)
    grad_blocks = grad_mixed.reshape(rows // block, block, heads, HEAD_DIM)
    starts = jnp.arange(rows // block, dtype=jnp.int32) * block
    key_heads = keys.reshape(count, heads, HEAD_DIM)
    value_heads = values.reshape(count, heads, HEAD_DIM)

    def one_block(carry, item):
        key_total, value_total = carry
        query_block, grad_block, block_totals, start = item
        scores = block_scores(query_block, key_heads, allowed_at(start, block), scale)
        probs = jnp.exp(scores - block_totals[..., None])
        value_total = value_total + jnp.einsum(
            "hqk,qhd->khd",
            probs.astype(jnp.bfloat16),
            grad_block,
            preferred_element_type=jnp.float32,
        )
        grad_probs = jnp.einsum(
            "qhd,khd->hqk", grad_block, value_heads, preferred_element_type=jnp.float32
        )
        inner = jnp.sum(grad_probs * probs, axis=-1, keepdims=True)
        grad_scores = (probs * (grad_probs - inner)).astype(jnp.bfloat16)
        grad_query = (
            jnp.einsum("hqk,khd->qhd", grad_scores, key_heads, preferred_element_type=jnp.float32)
            * scale
        )
        key_total = (
            key_total
            + jnp.einsum(
                "hqk,qhd->khd", grad_scores, query_block, preferred_element_type=jnp.float32
            )
            * scale
        )
        return ((key_total, value_total), grad_query.astype(jnp.bfloat16).reshape(block, cols))

    empty = jnp.zeros((count, heads, HEAD_DIM), jnp.float32)
    (key_total, value_total), grad_queries = lax.scan(
        one_block, (empty, empty), (query_blocks, grad_blocks, log_totals, starts)
    )
    return (
        grad_queries.reshape(rows, cols),
        key_total.reshape(count, cols).astype(jnp.bfloat16),
        value_total.reshape(count, cols).astype(jnp.bfloat16),
    )


def body(
    tokens,
    enc_states,
    utt_lengths,
    enc_lengths,
    self_qkv,
    self_out,
    cross_qkv,
    cross_out,
    ffn_proj,
    norm_gains,
    norm_biases,
    cotangent,
):
    local_rows = tokens.shape[0]
    rows = local_rows * lax.axis_size("tensor")
    block = min(512, rows)
    length = utt_lengths[0]
    enc_length = enc_lengths[0]
    offset = lax.axis_index("tensor") * local_rows
    positions = jnp.arange(rows, dtype=jnp.int32)
    full = (
        lax.all_gather(self_qkv, "dp", axis=1, tiled=True),
        lax.all_gather(self_out, "dp", axis=0, tiled=True),
        lax.all_gather(cross_qkv, "dp", axis=1, tiled=True),
        lax.all_gather(cross_out, "dp", axis=0, tiled=True),
        lax.all_gather(ffn_proj, "dp", axis=1, tiled=True),
        lax.all_gather(norm_gains, "dp", axis=1, tiled=True),
        lax.all_gather(norm_biases, "dp", axis=1, tiled=True),
    )
    self_in, self_back, cross_in, cross_back, ffn_full, gains_full, shifts_full = full
    gains = gains_full.astype(jnp.float32)
    shifts = shifts_full.astype(jnp.float32)

    def causal_at(start, size):
        query_pos = start + jnp.arange(size, dtype=jnp.int32)
        return (positions[None, :] <= query_pos[:, None]) & (positions[None, :] < length)

    start_x = tokens.astype(jnp.float32)
    normed1 = gather_rows(layer_norm(start_x, gains[0], shifts[0]).astype(jnp.bfloat16))
    self_proj = jnp.einsum(
        "rd,jdc->jrc", normed1, self_in, preferred_element_type=jnp.float32
    ).astype(jnp.bfloat16)
    mixed1, totals1 = attention_forward(self_proj[0], self_proj[1], self_proj[2], causal_at, block)
    first_x = start_x + sum_branch(
        jnp.einsum("rc,dc->rd", mixed1, self_back, preferred_element_type=jnp.float32)
    )
    normed2, enc_full = (
        lax.all_gather(
            layer_norm(first_x, gains[1], shifts[1]).astype(jnp.bfloat16),
            "tensor",
            axis=0,
            tiled=True,
        ),
        lax.all_gather(enc_states, "tensor", axis=0, tiled=True),
    )
    enc_count = enc_full.shape[0]
    enc_positions = jnp.arange(enc_count, dtype=jnp.int32)

    def cross_at(start, size):
        return jnp.broadcast_to((enc_positions < enc_length)[None, :], (size, enc_count))

    cross_query = jnp.dot(normed2, cross_in[0], preferred_element_type=jnp.float32).astype(
        jnp.bfloat16
    )
    cross_kv = jnp.einsum(
        "ed,jdc->jec", enc_full, cross_in[1:3], preferred_element_type=jnp.float32
    ).astype(jnp.bfloat16)
    mixed2, totals2 = attention_forward(cross_query, cross_kv[0], cross_kv[1], cross_at, block)
    second_x = first_x + sum_branch(
        jnp.einsum("rc,dc->rd", mixed2, cross_back, preferred_element_type=jnp.float32)
    )
    normed3 = gather_rows(layer_norm(second_x, gains[2], shifts[2]).astype(jnp.bfloat16))
    inner = jnp.dot(normed3, ffn_full[0], preferred_element_type=jnp.float32)
    active = gelu_tanh(inner).astype(jnp.bfloat16)
    third_x = second_x + sum_branch(
        jnp.einsum("rf,df->rd", active, ffn_full[1], preferred_element_type=jnp.float32)
    )
    output = layer_norm(third_x, gains[3], shifts[3]).astype(jnp.bfloat16)
    valid = (offset + jnp.arange(local_rows, dtype=jnp.int32) < length)[:, None]
    grad_out = cotangent.astype(jnp.float32) * valid
    grad_third, gain_last, shift_last = norm_back(third_x, gains[3], shifts[3], grad_out)
    grad_branch = gather_grads(grad_third.astype(jnp.bfloat16))
    down_grad = jnp.einsum("rd,rf->df", grad_branch, active, preferred_element_type=jnp.float32)
    grad_active = jnp.dot(grad_branch, ffn_full[1], preferred_element_type=jnp.float32)
    unused, gelu_pull = jax.vjp(gelu_tanh, inner)
    grad_inner = gelu_pull(grad_active)[0].astype(jnp.bfloat16)
    up_grad = jnp.einsum("rd,rf->df", normed3, grad_inner, preferred_element_type=jnp.float32)
    ffn_grad = jnp.stack([up_grad, down_grad])
    grad_normed3 = sum_inputs(
        jnp.einsum("rf,df->rd", grad_inner, ffn_full[0], preferred_element_type=jnp.float32)
    )
    back_x, gain_ffn, shift_ffn = norm_back(second_x, gains[2], shifts[2], grad_normed3)
    grad_second = grad_third + back_x
    grad_branch = gather_grads(grad_second.astype(jnp.bfloat16))
    cross_back_grad = jnp.einsum(
        "rd,rc->dc", grad_branch, mixed2, preferred_element_type=jnp.float32
    )
    grad_mixed2 = jnp.dot(grad_branch, cross_back, preferred_element_type=jnp.float32).astype(
        jnp.bfloat16
    )
    grad_cq, grad_ck, grad_cv = attention_backward(
        cross_query, cross_kv[0], cross_kv[1], grad_mixed2, totals2, cross_at, block
    )
    cross_in_grad = jnp.stack(
        [
            jnp.einsum("rd,rc->dc", normed2, grad_cq, preferred_element_type=jnp.float32),
            jnp.einsum("ed,ec->dc", enc_full, grad_ck, preferred_element_type=jnp.float32),
            jnp.einsum("ed,ec->dc", enc_full, grad_cv, preferred_element_type=jnp.float32),
        ]
    )
    grad_kv = jnp.stack([grad_ck, grad_cv])
    enc_part = jnp.einsum("jec,jdc->ed", grad_kv, cross_in[1:3], preferred_element_type=jnp.float32)
    normed_part = jnp.einsum("rc,dc->rd", grad_cq, cross_in[0], preferred_element_type=jnp.float32)
    grad_normed2, enc_grad = (
        lax.psum_scatter(
            normed_part.astype(jnp.bfloat16), "tensor", scatter_dimension=0, tiled=True
        ).astype(jnp.float32),
        lax.psum_scatter(
            enc_part.astype(jnp.bfloat16), "tensor", scatter_dimension=0, tiled=True
        ).astype(jnp.float32),
    )
    back_x, gain_cross, shift_cross = norm_back(first_x, gains[1], shifts[1], grad_normed2)
    grad_first = grad_second + back_x
    grad_branch = gather_grads(grad_first.astype(jnp.bfloat16))
    self_back_grad = jnp.einsum(
        "rd,rc->dc", grad_branch, mixed1, preferred_element_type=jnp.float32
    )
    grad_mixed1 = jnp.dot(grad_branch, self_back, preferred_element_type=jnp.float32).astype(
        jnp.bfloat16
    )
    grad_q, grad_k, grad_v = attention_backward(
        self_proj[0], self_proj[1], self_proj[2], grad_mixed1, totals1, causal_at, block
    )
    grad_proj = jnp.stack([grad_q, grad_k, grad_v])
    self_in_grad = jnp.einsum("rd,jrc->jdc", normed1, grad_proj, preferred_element_type=jnp.float32)
    grad_normed1 = sum_inputs(
        jnp.einsum("jrc,jdc->rd", grad_proj, self_in, preferred_element_type=jnp.float32)
    )
    back_x, gain_self, shift_self = norm_back(start_x, gains[0], shifts[0], grad_normed1)
    token_grad = grad_first + back_x
    summed = (
        lax.psum_scatter(self_in_grad, "dp", scatter_dimension=1, tiled=True),
        lax.psum_scatter(self_back_grad, "dp", scatter_dimension=0, tiled=True),
        lax.psum_scatter(cross_in_grad, "dp", scatter_dimension=1, tiled=True),
        lax.psum_scatter(cross_back_grad, "dp", scatter_dimension=0, tiled=True),
        lax.psum_scatter(ffn_grad, "dp", scatter_dimension=1, tiled=True),
    )
    self_in_sum, self_back_sum, cross_in_sum, cross_back_sum, ffn_sum = summed
    gain_terms = jnp.stack([gain_self, gain_cross, gain_ffn, gain_last])
    shift_terms = jnp.stack([shift_self, shift_cross, shift_ffn, shift_last])
    gains_grad, biases_grad = (
        lax.psum_scatter(gain_terms, ("dp", "tensor"), scatter_dimension=1, tiled=True),
        lax.psum_scatter(shift_terms, ("dp", "tensor"), scatter_dimension=1, tiled=True),
    )
    return (
        output,
        token_grad,
        enc_grad,
        self_in_sum,
        self_back_sum,
        cross_in_sum,
        cross_back_sum,
        ffn_sum,
        gains_grad,
        biases_grad,
    )


def solution(mesh):
    return jax.shard_map(
        body,
        mesh=mesh,
        in_specs=(
            P(("dp", "tensor"), None),
            P(("dp", "tensor"), None),
            P("dp"),
            P("dp"),
            P(None, "dp", "tensor"),
            P("dp", "tensor"),
            P(None, "dp", "tensor"),
            P("dp", "tensor"),
            P(None, "dp", "tensor"),
            P(None, "dp"),
            P(None, "dp"),
            P(("dp", "tensor"), None),
        ),
        out_specs=(
            P(("dp", "tensor"), None),
            P(("dp", "tensor"), None),
            P(("dp", "tensor"), None),
            P(None, "dp", "tensor"),
            P("dp", "tensor"),
            P(None, "dp", "tensor"),
            P("dp", "tensor"),
            P(None, "dp", "tensor"),
            P(None, ("dp", "tensor")),
            P(None, ("dp", "tensor")),
        ),
        check_vma=False,
    )
```

profile of v0, /device:TPU:0, one launch (start us, length us, event | category | flops | bytes accessed | tf_op | source)
XLA Modules:
  0.0 1868.4 jit_solution(317972658690794772)
XLA Ops:
  9.8 42.7 %all-gather = bf16[16,64,4]{1,2,0:T(4,128)(2,1)S(1)} all-gather(bf16[1,64,4]{1,2,0:T(4,128)(2,1)} %bitcast.239), channel_id=1, replica_groups=mesh['dp'=16,'tensor'=2] {'dp'}, dimensions={0}, use_global_device_ids=true | all-gather | bytes 8704 | tf_op jit(solution)/shard_map/all_gather | solution.py:159
  52.5 35.8 %all-gather.1 = bf16[16,64,4]{1,2,0:T(4,128)(2,1)S(1)} all-gather(bf16[1,64,4]{1,2,0:T(4,128)(2,1)} %bitcast.240), channel_id=1, replica_groups=mesh['dp'=16,'tensor'=2] {'dp'}, dimensions={0}, use_global_device_ids=true | all-gather | bytes 8704 | tf_op jit(solution)/shard_map/all_gather | solution.py:160
  97.4 71.6 %all-gather.16.cloned.1.call-done = bf16[3,1024,512]{2,1,0:T(8,128)(2,1)} async-done(((bf16[3,64,512]{2,1,0:T(8,128)(2,1)}), bf16[3,1024,512]{2,1,0:T(8,128)(2,1)}) %all-gather.16.cloned.1.call-update) | async-done | bytes 3145744 | tf_op jit(solution)/shard_map/all_gather | solution.py:154
  179.6 46.6 %all-gather.18.cloned.1.call-done = bf16[1024,512]{1,0:T(8,128)(2,1)} async-done(((bf16[64,512]{1,0:T(8,128)(2,1)}), bf16[1024,512]{1,0:T(8,128)(2,1)}) %all-gather.18.cloned.1.call-update) | async-done | bytes 1048592 | tf_op jit(solution)/shard_map/all_gather | solution.py:155
  229.8 6.9 reduce-scatter.18.cloned.1.call-done
  245.6 62.8 %all-gather.20.cloned.1.call-done = bf16[3,1024,512]{2,1,0:T(8,128)(2,1)} async-done(((bf16[3,64,512]{2,1,0:T(8,128)(2,1)}), bf16[3,1024,512]{2,1,0:T(8,128)(2,1)}) %all-gather.20.cloned.1.call-update) | async-done | bytes 3145744 | tf_op jit(solution)/shard_map/all_gather | solution.py:156
  310.9 7.8 all-gather.22.cloned.1.call-done
  324.8 53.4 %all-gather.24.cloned.1.call-done = bf16[1024,512]{1,0:T(8,128)(2,1)} async-done(((bf16[64,512]{1,0:T(8,128)(2,1)}), bf16[1024,512]{1,0:T(8,128)(2,1)}) %all-gather.24.cloned.1.call-update) | async-done | bytes 1048592 | tf_op jit(solution)/shard_map/all_gather | solution.py:157
  381.3 7.4 reduce-scatter.20.cloned.1.call-done
  392.1 9.7 all-gather.26.cloned.1.call-done
  401.8 116.5 %all-gather.28.cloned.1.call-done = bf16[2,1024,2048]{2,1,0:T(8,128)(2,1)} async-done(((bf16[2,64,2048]{2,1,0:T(8,128)(2,1)}), bf16[2,1024,2048]{2,1,0:T(8,128)(2,1)}) %all-gather.28.cloned.1.call-update) | async-done | bytes 8388624 | tf_op jit(solution)/shard_map/all_gather | solution.py:158
  529.0 6.8 reduce-scatter.22.cloned.1.call-done
  541.5 10.1 all-gather.30.cloned.1.call-done
  551.6 8.2 fusion.8
  561.1 5.5 fusion.31
  566.7 9.8 reduce-scatter.24.cloned.1.call-done
  582.3 10.3 all-gather.32.cloned.1.call-done
  604.4 9.6 reduce-scatter.26.cloned.1.call-done
  619.9 10.3 all-gather.34.cloned.1.call-done
  632.5 5.8 fusion.37
  638.3 5.4 multiply_reduce_fusion
  656.3 5.2 bitcast_convert_fusion
  678.5 5.7 convolution_bitcast_fusion.2
  684.2 9.4 copy.102
  714.7 6.0 pad_maximum_fusion
  726.2 93.9 %reduce-scatter.40.cloned.1.call-done = f32[32,4]{1,0:T(8,128)} async-done(((f32[1024,4]{1,0:T(8,128)}), f32[32,4]{1,0:T(8,128)}) %reduce-scatter.40.cloned.1.call-update) | async-done | bytes 528
  821.4 130.7 %reduce-scatter.42.cloned.1.call-done = f32[32,4]{1,0:T(8,128)} async-done(((f32[1024,4]{1,0:T(8,128)}), f32[32,4]{1,0:T(8,128)}) %reduce-scatter.42.cloned.1.call-update) | async-done | bytes 528
  953.4 258.2 %all-reduce.3.cloned.1.call-done = f32[3,1024,512]{2,0,1:T(4,128)} async-done(((f32[3,1024,512]{2,0,1:T(4,128)}), f32[3,1024,512]{2,0,1:T(4,128)}) %all-reduce.3.cloned.1.call-update) | async-done | bytes 6291472
  1213.7 80.3 %reduce-scatter.36.cloned.1.call-done = f32[64,512]{1,0:T(8,128)} async-done(((f32[1024,512]{1,0:T(8,128)}), f32[64,512]{1,0:T(8,128)}) %reduce-scatter.36.cloned.1.call-update) | async-done | bytes 131088 | tf_op jit(solution)/shard_map/reduce_scatter | solution.py:277
  1294.0 80.7 %reduce-scatter.32.cloned.1.call-done = f32[64,512]{1,0:T(8,128)} async-done(((f32[1024,512]{1,0:T(8,128)}), f32[64,512]{1,0:T(8,128)}) %reduce-scatter.32.cloned.1.call-update) | async-done | bytes 131088 | tf_op jit(solution)/shard_map/reduce_scatter | solution.py:275
  1374.7 136.2 %reduce-scatter.34.cloned.1.call-done = f32[3,64,512]{2,1,0:T(8,128)} async-done(((f32[3,1024,512]{2,1,0:T(8,128)}), f32[3,64,512]{2,1,0:T(8,128)}) %reduce-scatter.34.cloned.1.call-update) | async-done | bytes 393232 | tf_op jit(solution)/shard_map/reduce_scatter | solution.py:276
  1511.0 350.7 %reduce-scatter.38.cloned.1.call-done = f32[2,64,2048]{2,1,0:T(8,128)} async-done(((f32[2,1024,2048]{2,1,0:T(8,128)}), f32[2,64,2048]{2,1,0:T(8,128)}) %reduce-scatter.38.cloned.1.call-update) | async-done | bytes 1048592 | tf_op jit(solution)/shard_map/reduce_scatter | solution.py:278
  (238 shorter events, 151.3 us)
Async XLA Ops:
  7.2 90.3 %all-gather.14.cloned.1.call-start = ((), (), s32[]{:S(2)}) async-start(), calls=%async_computation.13 | async-start | bytes 1572864 | tf_op jit(solution)/shard_map/all_gather | solution.py:30
  90.6 78.4 %all-gather.16.cloned.1.call-start = ((), (), s32[]{:S(2)}) async-start(), calls=%async_computation.14 | async-start | bytes 3342336 | tf_op jit(solution)/shard_map/all_gather | solution.py:154
  91.3 134.8 %all-gather.18.cloned.1.call-start = ((), (), s32[]{:S(2)}) async-start(), calls=%async_computation.15 | async-start | bytes 1114112 | tf_op jit(solution)/shard_map/all_gather | solution.py:155
  92.1 144.6 %reduce-scatter.18.cloned.1.call-start = ((), (), s32[]{:S(2)}) async-start(), calls=%async_computation.16 | async-start | bytes 1572864 | tf_op jit(solution)/shard_map/reduce_scatter | solution.py:38
  179.6 61.9 %copy-start.26 = (bf16[8,64,512]{2,1,0:T(8,128)(2,1)}, bf16[8,64,512]{2,1,0:T(8,128)(2,1)S(1)}, u32[]{:S(2)}) copy-start(bf16[8,64,512]{2,1,0:T(8,128)(2,1)S(1)} %fusion.36) | copy-start | bytes 1572868
  179.6 57.1 %copy-start.3 = (bf16[256,1024]{1,0:T(8,128)(2,1)S(1)}, bf16[256,1024]{1,0:T(8,128)(2,1)}, u32[]{:S(2)}) copy-start(bf16[256,1024]{1,0:T(8,128)(2,1)} %param.12) | copy-start | bytes 1572868
  226.2 16.8 copy-start.31
  229.2 79.3 %all-gather.20.cloned.1.call-start = ((), (), s32[]{:S(2)}) async-start(), calls=%async_computation.17 | async-start | bytes 3342336 | tf_op jit(solution)/shard_map/all_gather | solution.py:156
  229.8 88.9 %all-gather.22.cloned.1.call-start = ((), (), s32[]{:S(2)}) async-start(), calls=%async_computation.18 | async-start | bytes 1572864 | tf_op jit(solution)/shard_map/all_gather | solution.py:180
  241.5 136.8 %all-gather.24.cloned.1.call-start = ((), (), s32[]{:S(2)}) async-start(), calls=%async_computation.19 | async-start | bytes 1114112 | tf_op jit(solution)/shard_map/all_gather | solution.py:157
  242.2 146.5 %reduce-scatter.20.cloned.1.call-start = ((), (), s32[]{:S(2)}) async-start(), calls=%async_computation.20 | async-start | bytes 1572864 | tf_op jit(solution)/shard_map/reduce_scatter | solution.py:38
  245.6 76.4 %copy-start.11 = (bf16[256,1024]{1,0:T(8,128)(2,1)}, bf16[256,1024]{1,0:T(8,128)(2,1)S(1)}, u32[]{:S(2)}) copy-start(bf16[256,1024]{1,0:T(8,128)(2,1)S(1)} %all_gather.48) | copy-start | bytes 1572868
  310.8 11.8 copy-start.25
  324.8 56.5 %copy-start.27 = (bf16[8,64,512]{2,1,0:T(8,128)(2,1)}, bf16[8,64,512]{2,1,0:T(8,128)(2,1)S(1)}, u32[]{:S(2)}) copy-start(bf16[8,64,512]{2,1,0:T(8,128)(2,1)S(1)} %fusion.35) | copy-start | bytes 1572868
  324.8 63.9 %copy-start.4 = (bf16[256,1024]{1,0:T(8,128)(2,1)S(1)}, bf16[256,1024]{1,0:T(8,128)(2,1)}, u32[]{:S(2)}) copy-start(bf16[256,1024]{1,0:T(8,128)(2,1)} %reduce-scatter.18.cloned.1.call-done) | copy-start | bytes 1572868
  381.2 20.5 %all-gather.26.cloned.1.call-start = ((), (), s32[]{:S(2)}) async-start(), calls=%async_computation.21 | async-start | bytes 1572864 | tf_op jit(solution)/shard_map/all_gather | solution.py:30
  391.4 126.9 %all-gather.28.cloned.1.call-start = ((), (), s32[]{:S(2)}) async-start(), calls=%async_computation.22 | async-start | bytes 8912896 | tf_op jit(solution)/shard_map/all_gather | solution.py:158
  392.0 143.9 %reduce-scatter.22.cloned.1.call-start = ((), (), s32[]{:S(2)}) async-start(), calls=%async_computation.23 | async-start | bytes 1572864 | tf_op jit(solution)/shard_map/reduce_scatter | solution.py:38
  529.0 22.7 %all-gather.30.cloned.1.call-start = ((), (), s32[]{:S(2)}) async-start(), calls=%async_computation.24 | async-start | bytes 1572864 | tf_op jit(solution)/shard_map/all_gather | solution.py:34
  541.3 35.2 %reduce-scatter.24.cloned.1.call-start = ((), (), s32[]{:S(2)}) async-start(), calls=%async_computation.25 | async-start | bytes 1572864 | tf_op jit(solution)/shard_map/reduce_scatter | solution.py:44
  566.7 25.9 %all-gather.32.cloned.1.call-start = ((), (), s32[]{:S(2)}) async-start(), calls=%async_computation.26 | async-start | bytes 1572864 | tf_op jit(solution)/shard_map/all_gather | solution.py:34
  582.2 31.8 %reduce-scatter.26.cloned.1.call-start = ((), (), s32[]{:S(2)}) async-start(), calls=%async_computation.27 | async-start | bytes 1572864 | tf_op jit(solution)/shard_map/reduce_scatter | solution.py:247
  604.1 26.0 %all-gather.34.cloned.1.call-start = ((), (), s32[]{:S(2)}) async-start(), calls=%async_computation.28 | async-start | bytes 1572864 | tf_op jit(solution)/shard_map/all_gather | solution.py:34
  619.8 53.3 %reduce-scatter.28.cloned.1.call-start = ((), (), s32[]{:S(2)}) async-start(), calls=%async_computation.29 | async-start | bytes 1572864 | tf_op jit(solution)/shard_map/reduce_scatter | solution.py:44
  661.5 61.1 %reduce-scatter.30.cloned.1.call-start = ((), (), s32[]{:S(2)}) async-start(), calls=%async_computation.30 | async-start | bytes 786432 | tf_op jit(solution)/shard_map/reduce_scatter | solution.py:250
  672.6 147.4 %reduce-scatter.40.cloned.1.call-start = ((), (), s32[]{:S(2)}) async-start(), calls=%async_computation.35 | async-start | bytes 540672
  677.3 274.8 %reduce-scatter.42.cloned.1.call-start = ((), (), s32[]{:S(2)}) async-start(), calls=%async_computation.36 | async-start | bytes 540672
  678.4 533.2 %all-reduce.3.cloned.1.call-start = ((), (), s32[]{:S(2)}) async-start(), calls=%async_computation.37 | async-start | bytes 16777216
  693.7 600.3 %reduce-scatter.36.cloned.1.call-start = ((), (), s32[]{:S(2)}) async-start(), calls=%async_computation.33 | async-start | bytes 2228224 | tf_op jit(solution)/shard_map/reduce_scatter | solution.py:277
  698.1 676.7 %reduce-scatter.32.cloned.1.call-start = ((), (), s32[]{:S(2)}) async-start(), calls=%async_computation.31 | async-start | bytes 2228224 | tf_op jit(solution)/shard_map/reduce_scatter | solution.py:275
  701.3 809.6 %reduce-scatter.34.cloned.1.call-start = ((), (), s32[]{:S(2)}) async-start(), calls=%async_computation.32 | async-start | bytes 6684672 | tf_op jit(solution)/shard_map/reduce_scatter | solution.py:276
  706.8 1154.9 %reduce-scatter.38.cloned.1.call-start = ((), (), s32[]{:S(2)}) async-start(), calls=%async_computation.34 | async-start | bytes 17825792 | tf_op jit(solution)/shard_map/reduce_scatter | solution.py:278
  (34 other events, 131.9 us)
Sparse Core Ops, SparseCore 0:
  90.7 6.7 all-gather.13
  100.2 68.7 all-gather.15
  171.8 54.3 all-gather.17
  229.3 7.3 reduce-scatter.17
  239.7 68.7 all-gather.19
  310.5 8.1 all-gather.21
  321.8 56.4 all-gather.23
  381.4 7.3 reduce-scatter.19
  391.5 10.1 all-gather.25
  404.4 113.8 all-gather.27
  529.1 6.7 reduce-scatter.21
  541.4 10.1 all-gather.29
  566.8 9.6 reduce-scatter.23
  582.3 10.1 all-gather.31
  604.3 9.6 reduce-scatter.25
  619.9 10.1 all-gather.33
  661.6 9.6 reduce-scatter.27
  673.4 9.1 reduce-scatter.29
  684.9 135.0 reduce-scatter.39
  822.1 129.9 reduce-scatter.41
  959.1 252.4 all-reduce.2
  1214.6 79.3 reduce-scatter.35
  1296.9 77.7 reduce-scatter.31
  1377.5 133.3 reduce-scatter.33
  1513.9 347.7 reduce-scatter.37
where the time goes:
time: 1880 us; the launch traced here: 1870 us
  waiting for transfers between devices  1580 us (84%)
  matrix products  103 us (5%)
  blocking collectives  81.2 us (4%)
  other arithmetic  50.6 us (3%)
  local copies, waits for them, and re-layouts  36.2 us (2%)
    unnamed x28, waiting for transfers between devices  486 us
    reduce_scatter x1, waiting for transfers between devices, body(): lax.psum_scatter(ffn_grad, 'dp', scatter_dimension=1, tiled=True)  351 us
    reduce_scatter x1, waiting for transfers between devices, body(): lax.psum_scatter(cross_in_grad, 'dp', scatter_dimension=1, tiled=True)  136 us
    all_gather x1, waiting for transfers between devices, body(): lax.all_gather(ffn_proj, 'dp', axis=1, tiled=True)  117 us
    reduce_scatter x1, waiting for transfers between devices, body(): lax.psum_scatter(self_back_grad, 'dp', scatter_dimension=0, tiled=True)  80.7 us
    reduce_scatter x1, waiting for transfers between devices, body(): lax.psum_scatter(cross_back_grad, 'dp', scatter_dimension=0, tiled=True)  80.3 us
    all_gather x1, waiting for transfers between devices, body(): lax.all_gather(self_qkv, 'dp', axis=1, tiled=True)  71.6 us
    all_gather x1, waiting for transfers between devices, body(): lax.all_gather(cross_qkv, 'dp', axis=1, tiled=True)  62.8 us
  transfers between devices with their start and end apart: 25, of which 23 were waited for; matrix products, arithmetic and copies ran while one was open for 5% of the time, Pallas kernels for 0%

commit v1 on v0

v1 whole, which is shorter than its diff:
```python
import jax
import jax.numpy as jnp
from jax import lax
from jax.sharding import PartitionSpec as P

HEAD_DIM = 64
EPSILON = 1e-05
NEG_FILL = -1000000000.0
BF = jnp.bfloat16
F32 = jnp.float32


def dot(a, b, dims):
    return lax.dot_general(a, b, (dims, ((), ())), preferred_element_type=F32)


def mm(a, b):
    return dot(a, b, ((1,), (0,)))


def mm_t(a, b):
    return dot(a, b, ((1,), (1,)))


def t_mm(a, b):
    return dot(a, b, ((0,), (0,)))


def swap(values):
    return lax.ppermute(values, "tensor", [(0, 1), (1, 0)])


def normalize(values):
    centre = jnp.mean(values, axis=-1, keepdims=True)
    centred = values - centre
    spread = jnp.mean(centred * centred, axis=-1, keepdims=True)
    rstd = lax.rsqrt(spread + EPSILON)
    return centred * rstd, rstd


def norm_back(hat, rstd, gain, grad):
    scaled = grad * gain
    first = jnp.mean(scaled, axis=-1, keepdims=True)
    second = jnp.mean(scaled * hat, axis=-1, keepdims=True)
    return (
        rstd * (scaled - first - hat * second),
        jnp.sum(grad * hat, axis=0),
        jnp.sum(grad, axis=0),
    )


def gelu_both(z):
    c = 0.7978845608028654
    t = jnp.tanh(c * (z + 0.044715 * z * z * z))
    value = 0.5 * z * (1.0 + t)
    slope = 0.5 * (1.0 + t) + 0.5 * z * (1.0 - t * t) * c * (1.0 + 3.0 * 0.044715 * z * z)
    return value, slope


def heads_of(values):
    rows, cols = values.shape
    return values.reshape(rows, cols // HEAD_DIM, HEAD_DIM)


def attend(q, k, v, allowed):
    scale = HEAD_DIM ** (-0.5)
    scores = (
        jnp.einsum("qhd,khd->hqk", heads_of(q), heads_of(k), preferred_element_type=F32) * scale
    )
    scores = jnp.where(allowed[None], scores, NEG_FILL)
    top = jnp.max(scores, axis=-1, keepdims=True)
    exps = jnp.exp(scores - top)
    total = jnp.sum(exps, axis=-1, keepdims=True)
    weights = (exps / total).astype(BF)
    mixed = jnp.einsum("hqk,khd->qhd", weights, heads_of(v), preferred_element_type=F32)
    return mixed.astype(BF).reshape(q.shape), top + jnp.log(total)


def attend_back(q, k, v, grad, logs, allowed):
    scale = HEAD_DIM ** (-0.5)
    qh, kh, vh, gh = heads_of(q), heads_of(k), heads_of(v), heads_of(grad)
    scores = jnp.einsum("qhd,khd->hqk", qh, kh, preferred_element_type=F32) * scale
    scores = jnp.where(allowed[None], scores, NEG_FILL)
    probs = jnp.exp(scores - logs)
    dv = jnp.einsum("hqk,qhd->khd", probs.astype(BF), gh, preferred_element_type=F32)
    dprobs = jnp.einsum("qhd,khd->hqk", gh, vh, preferred_element_type=F32)
    inner = jnp.sum(dprobs * probs, axis=-1, keepdims=True)
    ds = (probs * (dprobs - inner)).astype(BF)
    dq = jnp.einsum("hqk,khd->qhd", ds, kh, preferred_element_type=F32) * scale
    dk = jnp.einsum("hqk,qhd->khd", ds, qh, preferred_element_type=F32) * scale
    return (
        dq.astype(BF).reshape(q.shape),
        dk.astype(BF).reshape(k.shape),
        dv.astype(BF).reshape(v.shape),
    )


def make_body(n_dp):
    bits = n_dp.bit_length() - 1
    assert n_dp == 1 << bits

    def hop(values, bit):
        return lax.ppermute(values, "dp", [(i, i ^ (1 << bit)) for i in range(n_dp)])

    far = tuple(range(bits - 1, 1, -1))
    gather_a = far + (1, 0)
    gather_b = far + (0, 1)
    gather_c = (0, 1) + far
    gather_d = (1, 0) + far
    scatter_a, scatter_b, scatter_c, scatter_d = (
        order[::-1] for order in (gather_a, gather_b, gather_c, gather_d)
    )

    def gather(shard, order):
        lead, feats, *rest = shard.shape
        held = shard.reshape((lead,) + (1,) * bits + (feats, *rest))
        for bit in order:
            held = jnp.concatenate([held, hop(held, bit)], axis=1 + bit)
        return held.reshape(lead, n_dp * feats, *rest)

    def scatter(full, order, kind):
        lead, feats, *rest = full.shape
        held = full.reshape((lead,) + (2,) * bits + (feats // n_dp, *rest))
        for count, bit in enumerate(order):
            keep = lax.slice_in_dim(held, 0, 1, axis=1 + bit)
            send = lax.slice_in_dim(held, 1, 2, axis=1 + bit)
            total = keep.astype(F32) + hop(send, bit).astype(F32)
            held = total.astype(F32 if count == bits - 1 else kind)
        return held.reshape(lead, feats // n_dp, *rest)

    def body(
        tokens,
        enc_states,
        utt_lengths,
        enc_lengths,
        self_qkv,
        self_out,
        cross_qkv,
        cross_out,
        ffn_proj,
        norm_gains,
        norm_biases,
        cotangent,
    ):
        local, width = tokens.shape
        enc_local = enc_states.shape[0]
        rows = 2 * local
        count = 2 * enc_local
        units = ffn_proj.shape[2]
        half = units // 2
        length = utt_lengths[0]
        enc_length = enc_lengths[0]
        core = lax.axis_index("tensor")
        me = lax.axis_index("dp")

        block = width // n_dp
        cols = jnp.arange(width, dtype=jnp.int32)
        labels = cols // block
        reverse = jnp.zeros_like(labels)
        for bit in range(bits):
            reverse = reverse | (((labels >> (bits - 1 - bit)) & 1) << bit)
        source = (me ^ reverse) * block + cols % block
        relabel = (cols[:, None] == source[None, :]).astype(BF)

        params = jnp.concatenate([norm_gains, norm_biases])
        params = gather(params.astype(BF), gather_a).astype(F32)
        gains, shifts = params[:4], params[4:]

        w_qk = gather(self_qkv[:2], gather_a)
        w_vo = gather(jnp.stack([self_qkv[2], self_out]), gather_b)
        c_kv = gather(cross_qkv[1:], gather_a)
        c_qo = gather(jnp.stack([cross_qkv[0], cross_out]), gather_b)
        up = [
            gather(ffn_proj[:1, :, :half], gather_a)[0],
            gather(ffn_proj[:1, :, half:], gather_b)[0],
        ]
        down = [
            gather(ffn_proj[1:, :, :half], gather_c)[0],
            gather(ffn_proj[1:, :, half:], gather_d)[0],
        ]

        def whole(mine):
            other = swap(mine)
            return jnp.where(
                core == 0,
                jnp.concatenate([mine, other]),
                jnp.concatenate([other, mine]),
            )

        def relabeled(values):
            return mm(values, relabel).astype(BF)

        def own(values):
            size = values.shape[0] // 2
            return lax.dynamic_slice_in_dim(values, core * size, size)

        def other(values):
            size = values.shape[0] // 2
            return lax.dynamic_slice_in_dim(values, (1 - core) * size, size)

        def restored(values):
            return lax.dot_general(
                values,
                relabel.astype(F32),
                (((1,), (1,)), ((), ())),
                precision=lax.Precision.HIGHEST,
                preferred_element_type=F32,
            )

        def both(part):
            mine = part.astype(BF)
            return mine.astype(F32) + swap(mine).astype(F32)

        x0 = whole(relabeled(tokens)).astype(F32)
        enc = whole(relabeled(enc_states))
        cot = whole(relabeled(cotangent)).astype(F32)

        position = jnp.arange(rows, dtype=jnp.int32)
        enc_position = jnp.arange(count, dtype=jnp.int32)
        causal = (position[None, :] <= position[:, None]) & (position[None, :] < length)
        reach = jnp.broadcast_to((enc_position < enc_length)[None, :], (rows, count))

        hat0, rstd0 = normalize(x0)
        normed1 = (hat0 * gains[0] + shifts[0]).astype(BF)
        q1 = mm(normed1, w_qk[0]).astype(BF)
        k1 = mm(normed1, w_qk[1]).astype(BF)
        v1 = mm(normed1, w_vo[0]).astype(BF)
        o1, logs1 = attend(q1, k1, v1, causal)
        x1 = x0 + both(mm_t(o1, w_vo[1]))
        hat1, rstd1 = normalize(x1)
        normed2 = (hat1 * gains[1] + shifts[1]).astype(BF)
        k2 = mm(enc, c_kv[0]).astype(BF)
        v2 = mm(enc, c_kv[1]).astype(BF)
        q2 = mm(normed2, c_qo[0]).astype(BF)
        o2, logs2 = attend(q2, k2, v2, reach)
        x2 = x1 + both(mm_t(o2, c_qo[1]))
        hat2, rstd2 = normalize(x2)
        normed3 = (hat2 * gains[2] + shifts[2]).astype(BF)
        acts, slopes = [], []
        for w in up:
            value, slope = gelu_both(mm(normed3, w))
            acts.append(value.astype(BF))
            slopes.append(slope)
        x3 = x2 + both(mm_t(acts[0], down[0]) + mm_t(acts[1], down[1]))
        hat3, rstd3 = normalize(x3)
        output = restored(own(hat3 * gains[3] + shifts[3]).astype(BF).astype(F32)).astype(BF)
        gout = cot * (position < length)[:, None]
        dx3, dgain3, dshift3 = norm_back(hat3, rstd3, gains[3], gout)
        dy3 = dx3.astype(BF)
        d_down = [t_mm(dy3, a).astype(BF)[None] for a in acts]
        s_down = [scatter(d_down[0], scatter_c, BF), scatter(d_down[1], scatter_d, BF)]
        dus = [(mm(dy3, w) * s).astype(BF) for w, s in zip(down, slopes)]
        d_up = [t_mm(normed3, du).astype(BF)[None] for du in dus]
        s_up = [scatter(d_up[0], scatter_a, BF), scatter(d_up[1], scatter_b, BF)]
        dn3 = both(mm_t(dus[0], up[0]) + mm_t(dus[1], up[1]))
        back, dgain2, dshift2 = norm_back(hat2, rstd2, gains[2], dn3)
        dx2 = dx3 + back
        dy2 = dx2.astype(BF)
        d_cross_out = t_mm(dy2, o2).astype(BF)
        do2 = mm(dy2, c_qo[1]).astype(BF)
        dq2, dk2, dv2 = attend_back(q2, k2, v2, do2, logs2, reach)
        s_qo = scatter(jnp.stack([t_mm(normed2, dq2).astype(BF), d_cross_out]), scatter_a, BF)
        s_kv = scatter(
            jnp.stack([t_mm(enc, dk2).astype(BF), t_mm(enc, dv2).astype(BF)]), scatter_b, BF
        )
        enc_part = mm_t(dk2, c_kv[0]) + mm_t(dv2, c_kv[1])
        enc_grad = restored(own(enc_part) + swap(other(enc_part).astype(BF)).astype(F32))
        dn2 = both(mm_t(dq2, c_qo[0]))
        back, dgain1, dshift1 = norm_back(hat1, rstd1, gains[1], dn2)
        dx1 = dx2 + back
        dy1 = dx1.astype(BF)
        d_self_out = t_mm(dy1, o1).astype(BF)
        do1 = mm(dy1, w_vo[1]).astype(BF)
        dq1, dk1, dv1 = attend_back(q1, k1, v1, do1, logs1, causal)
        t_vo = scatter(jnp.stack([t_mm(normed1, dv1).astype(BF), d_self_out]), scatter_a, BF)
        t_qk = scatter(
            jnp.stack([t_mm(normed1, dq1).astype(BF), t_mm(normed1, dk1).astype(BF)]),
            scatter_b,
            BF,
        )
        dn1 = both(mm_t(dq1, w_qk[0]) + mm_t(dk1, w_qk[1]) + mm_t(dv1, w_vo[0]))
        back, dgain0, dshift0 = norm_back(hat0, rstd0, gains[0], dn1)
        token_grad = restored(own(dx1 + back))

        terms = jnp.stack(
            [dgain0, dgain1, dgain2, dgain3, dshift0, dshift1, dshift2, dshift3]
        )
        terms = scatter(terms, scatter_a, F32)
        part = terms.shape[1] // 2
        terms = lax.dynamic_slice_in_dim(terms, core * part, part, axis=1)
        return (
            output,
            token_grad,
            enc_grad,
            jnp.concatenate([t_qk, t_vo[:1]]),
            t_vo[1],
            jnp.concatenate([s_qo[:1], s_kv]),
            s_qo[1],
            jnp.concatenate(
                [jnp.concatenate(s_up, axis=2), jnp.concatenate(s_down, axis=2)]
            ),
            terms[:4],
            terms[4:],
        )

    return body


def solution(mesh):
    return jax.shard_map(
        make_body(mesh.shape["dp"]),
        mesh=mesh,
        in_specs=(
            P(("dp", "tensor"), None),
            P(("dp", "tensor"), None),
            P("dp"),
            P("dp"),
            P(None, "dp", "tensor"),
            P("dp", "tensor"),
            P(None, "dp", "tensor"),
            P("dp", "tensor"),
            P(None, "dp", "tensor"),
            P(None, "dp"),
            P(None, "dp"),
            P(("dp", "tensor"), None),
        ),
        out_specs=(
            P(("dp", "tensor"), None),
            P(("dp", "tensor"), None),
            P(("dp", "tensor"), None),
            P(None, "dp", "tensor"),
            P("dp", "tensor"),
            P(None, "dp", "tensor"),
            P("dp", "tensor"),
            P(None, "dp", "tensor"),
            P(None, ("dp", "tensor")),
            P(None, ("dp", "tensor")),
        ),
        check_vma=False,
    )
```

time: 1880 us -> 552 us (0.29)
  waiting for transfers between devices: 1580 us -> 261 us
  blocking collectives: 81.2 us -> 0 us
  starting transfers between devices: 1.98 us -> 80.9 us
  other arithmetic: 50.6 us -> 77.2 us
  matrix products: 103 us -> 80.7 us
    reduce_scatter x11 -> x0, waiting for transfers between devices: 689 us -> none  [the longest x1 351 us: body(): lax.psum_scatter(ffn_grad, 'dp', scatter_dimension=1, tiled=True)]
    unnamed x28 -> x0, waiting for transfers between devices: 486 us -> none
    all_gather x11 -> x0, waiting for transfers between devices: 404 us -> none  [the longest x1 117 us: body(): lax.all_gather(ffn_proj, 'dp', axis=1, tiled=True)]
    ppermute x0 -> x82, waiting for transfers between devices: none -> 261 us  [the longest x72 261 us: hop(): return lax.ppermute(values, 'dp', [(i, i ^ 1 << bit) for i in range(n_dp)])]
    all_gather x3 -> x0, blocking collectives: 81.2 us -> none  [the longest x1 42.7 us: body(): lax.all_gather(norm_gains, 'dp', axis=1, tiled=True)]
    ppermute x0 -> x82, starting transfers between devices: none -> 80.9 us  [the longest x72 79.7 us: hop(): return lax.ppermute(values, 'dp', [(i, i ^ 1 << bit) for i in range(n_dp)])]
    dot_general x34 -> x54, matrix products: 103 us -> 80.7 us  [the longest x39 53.2 us: dot(): return lax.dot_general(a, b, (dims, ((), ())), preferred_element_type=F32)]
  transfers between devices with their start and end apart: 25 -> 82, of which waited for: 23 -> 38; matrix products, arithmetic and copies ran while one was open for 5% -> 28% of each run, Pallas kernels for 0% -> 0%
where the time goes in v1:
time: 552 us; the launch traced here: 542 us
  waiting for transfers between devices  261 us (47%)
  starting transfers between devices  80.9 us (15%)
  matrix products  80.7 us (15%)
  other arithmetic  77.2 us (14%)
  local copies, waits for them, and re-layouts  36.9 us (7%)
    ppermute x72, waiting for transfers between devices, hop(): return lax.ppermute(values, 'dp', [(i, i ^ 1 << bit) for i in range(n_dp)])  261 us
    ppermute x72, starting transfers between devices, hop(): return lax.ppermute(values, 'dp', [(i, i ^ 1 << bit) for i in range(n_dp)])  79.7 us
    dot_general x39, matrix products, dot(): return lax.dot_general(a, b, (dims, ((), ())), preferred_element_type=F32)  53.2 us
    concatenate x35, other arithmetic, gather(): held = jnp.concatenate([held, hop(held, bit)], axis=1 + bit)  16.2 us
    convert_element_type x24, other arithmetic, scatter(): held = total.astype(F32 if count == bits - 1 else kind)  15.8 us
    unnamed x316, local copies, waits for them, and re-layouts  14.3 us
  transfers between devices with their start and end apart: 82, of which 38 were waited for; matrix products, arithmetic and copies ran while one was open for 28% of the time, Pallas kernels for 0%

profile of v1, /device:TPU:0, one launch (start us, length us, event | category | flops | bytes accessed | tf_op | source)
XLA Modules:
  0.0 542.1 jit_solution(5900806302516893984)
XLA Ops:
  1.4 4.1 collective-permute-start.1
  38.2 3.0 collective-permute-start.32
  44.2 3.1 collective-permute-start.16
  49.7 10.4 %collective-permute-done.6 = bf16[2,1,1,1,2,64,512]{6,5,0,4,3,2,1:T(8,128)(2,1)S(1)} collective-permute-done((bf16[2,1,1,1,2,64,512]{6,5,0,4,3,2,1:T(8,128)(2,1)S(1)}, bf16[2,1,1,1,2,64,512]{6,5,0,4,3,2,1:T(8,128)(2,1)S(1)}, u32[]{:S(2)}, u32[]{:S(2)}) %collective-permute-start.6) | collective-permute-done | bytes 262176 | tf_op jit(solution)/shard_map/ppermute | solution.py:103
  62.2 3.5 collective-permute-done.20
  65.8 5.6 %collective-permute-done.10 = bf16[2,1,1,1,2,64,512]{6,5,0,4,3,2,1:T(8,128)(2,1)S(1)} collective-permute-done((bf16[2,1,1,1,2,64,512]{6,5,0,4,3,2,1:T(8,128)(2,1)S(1)}, bf16[2,1,1,1,2,64,512]{6,5,0,4,3,2,1:T(8,128)(2,1)S(1)}, u32[]{:S(2)}, u32[]{:S(2)}) %collective-permute-start.10) | collective-permute-done | bytes 262176 | tf_op jit(solution)/shard_map/ppermute | solution.py:103
  79.2 6.1 %collective-permute-done.37 = bf16[1,1,2,1,1,64,1024]{6,5,4,3,2,1,0:T(8,128)(2,1)S(1)} collective-permute-done((bf16[1,1,2,1,1,64,1024]{6,5,4,3,2,1,0:T(8,128)(2,1)S(1)}, bf16[1,1,2,1,1,64,1024]{6,5,4,3,2,1,0:T(8,128)(2,1)S(1)}, u32[]{:S(2)}, u32[]{:S(2)}) %collective-permute-start.37) | collective-permute-done | bytes 262176 | tf_op jit(solution)/shard_map/ppermute | solution.py:103
  88.4 18.1 %collective-permute-done.11 = bf16[2,1,1,2,2,64,512]{6,5,0,4,3,2,1:T(8,128)(2,1)S(1)} collective-permute-done((bf16[2,1,1,2,2,64,512]{6,5,0,4,3,2,1:T(8,128)(2,1)S(1)}, bf16[2,1,1,2,2,64,512]{6,5,0,4,3,2,1:T(8,128)(2,1)S(1)}, u32[]{:S(2)}, u32[]{:S(2)}) %collective-permute-start.11) | collective-permute-done | bytes 524320 | tf_op jit(solution)/shard_map/ppermute | solution.py:103
  114.9 23.3 %collective-permute-done.30 = bf16[1,2,2,1,1,64,1024]{6,5,4,3,2,1,0:T(8,128)(2,1)S(1)} collective-permute-done((bf16[1,2,2,1,1,64,1024]{6,5,4,3,2,1,0:T(8,128)(2,1)S(1)}, bf16[1,2,2,1,1,64,1024]{6,5,4,3,2,1,0:T(8,128)(2,1)S(1)}, u32[]{:S(2)}, u32[]{:S(2)}) %collective-permute-start.30) | collective-permute-done | bytes 524320 | tf_op jit(solution)/shard_map/ppermute | solution.py:103
  141.1 8.2 %collective-permute-done.38 = bf16[1,2,2,1,1,64,1024]{6,5,4,3,2,1,0:T(8,128)(2,1)S(1)} collective-permute-done((bf16[1,2,2,1,1,64,1024]{6,5,4,3,2,1,0:T(8,128)(2,1)S(1)}, bf16[1,2,2,1,1,64,1024]{6,5,4,3,2,1,0:T(8,128)(2,1)S(1)}, u32[]{:S(2)}, u32[]{:S(2)}) %collective-permute-start.38) | collective-permute-done | bytes 524320 | tf_op jit(solution)/shard_map/ppermute | solution.py:103
  156.5 21.8 %collective-permute-done.8 = bf16[2,2,1,2,2,64,512]{6,5,0,4,3,2,1:T(8,128)(2,1)S(1)} collective-permute-done((bf16[2,2,1,2,2,64,512]{6,5,0,4,3,2,1:T(8,128)(2,1)S(1)}, bf16[2,2,1,2,2,64,512]{6,5,0,4,3,2,1:T(8,128)(2,1)S(1)}, u32[]{:S(2)}, u32[]{:S(2)}) %collective-permute-start.8) | collective-permute-done | bytes 1048608 | tf_op jit(solution)/shard_map/ppermute | solution.py:103
  187.0 15.0 %collective-permute-done.18 = bf16[2,1,2,2,2,64,512]{6,5,0,4,3,2,1:T(8,128)(2,1)S(1)} collective-permute-done((bf16[2,1,2,2,2,64,512]{6,5,0,4,3,2,1:T(8,128)(2,1)S(1)}, bf16[2,1,2,2,2,64,512]{6,5,0,4,3,2,1:T(8,128)(2,1)S(1)}, u32[]{:S(2)}, u32[]{:S(2)}) %collective-permute-start.18) | collective-permute-done | bytes 1048608 | tf_op jit(solution)/shard_map/ppermute | solution.py:103
  213.2 12.1 %collective-permute-done.22 = bf16[2,2,1,2,2,64,512]{6,5,0,4,3,2,1:T(8,128)(2,1)} collective-permute-done((bf16[2,2,1,2,2,64,512]{6,5,0,4,3,2,1:T(8,128)(2,1)}, bf16[2,2,1,2,2,64,512]{6,5,0,4,3,2,1:T(8,128)(2,1)}, u32[]{:S(2)}, u32[]{:S(2)}) %collective-permute-start.22) | collective-permute-done | bytes 1048608 | tf_op jit(solution)/shard_map/ppermute | solution.py:103
  266.5 4.2 multiply_reduce_fusion.2
  270.7 3.0 fusion.125
  299.9 12.4 %collective-permute-done.74 = bf16[1,2,2,1,2,64,1024]{6,5,4,3,2,1,0:T(8,128)(2,1)} collective-permute-done((bf16[1,2,2,1,2,64,1024]{6,5,4,3,2,1,0:T(8,128)(2,1)}, bf16[1,2,2,1,2,64,1024]{6,5,4,3,2,1,0:T(8,128)(2,1)}, u32[]{:S(2)}, u32[]{:S(2)}) %collective-permute-start.74) | collective-permute-done | bytes 1048608 | tf_op jit(solution)/shard_map/ppermute | solution.py:103
  316.5 28.7 %collective-permute-done.70 = bf16[1,2,2,1,2,64,1024]{6,5,4,3,2,1,0:T(8,128)(2,1)} collective-permute-done((bf16[1,2,2,1,2,64,1024]{6,5,4,3,2,1,0:T(8,128)(2,1)}, bf16[1,2,2,1,2,64,1024]{6,5,4,3,2,1,0:T(8,128)(2,1)}, u32[]{:S(2)}, u32[]{:S(2)}) %collective-permute-start.70) | collective-permute-done | bytes 1048608 | tf_op jit(solution)/shard_map/ppermute | solution.py:103
  349.4 3.7 multiply_add_fusion.3
  376.6 4.3 fusion.5
  389.0 22.7 %collective-permute-done.76 = bf16[1,1,2,1,1,64,1024]{6,5,4,3,2,1,0:T(8,128)(2,1)S(1)} collective-permute-done((bf16[1,1,2,1,1,64,1024]{6,5,4,3,2,1,0:T(8,128)(2,1)S(1)}, bf16[1,1,2,1,1,64,1024]{6,5,4,3,2,1,0:T(8,128)(2,1)S(1)}, u32[]{:S(2)}, u32[]{:S(2)}) %collective-permute-start.76) | collective-permute-done | bytes 262176 | tf_op jit(solution)/shard_map/ppermute | solution.py:103
  414.5 6.9 %collective-permute-done.64 = bf16[1,1,1,1,2,64,1024]{6,5,4,3,2,1,0:T(8,128)(2,1)S(1)} collective-permute-done((bf16[1,1,1,1,2,64,1024]{6,5,4,3,2,1,0:T(8,128)(2,1)S(1)}, bf16[1,1,1,1,2,64,1024]{6,5,4,3,2,1,0:T(8,128)(2,1)S(1)}, u32[]{:S(2)}, u32[]{:S(2)}) %collective-permute-start.64) | collective-permute-done | bytes 262176 | tf_op jit(solution)/shard_map/ppermute | solution.py:103
  422.0 3.4 collective-permute-done.68
  431.2 6.4 %collective-permute-done.65 = bf16[1,1,1,1,1,64,1024]{6,5,4,3,2,1,0:T(8,128)(2,1)S(1)} collective-permute-done((bf16[1,1,1,1,1,64,1024]{6,5,4,3,2,1,0:T(8,128)(2,1)S(1)}, bf16[1,1,1,1,1,64,1024]{6,5,4,3,2,1,0:T(8,128)(2,1)S(1)}, u32[]{:S(2)}, u32[]{:S(2)}) %collective-permute-start.65) | collective-permute-done | bytes 131104 | tf_op jit(solution)/shard_map/ppermute | solution.py:103
  472.9 3.3 collective-permute-done.55
  478.4 3.4 collective-permute-done.60
  482.0 4.0 collective-permute-done.56
  486.2 6.4 %collective-permute-done.61 = bf16[2,1,1,1,1,64,512]{6,5,0,4,3,2,1:T(8,128)(2,1)S(1)} collective-permute-done((bf16[2,1,1,1,1,64,512]{6,5,0,4,3,2,1:T(8,128)(2,1)S(1)}, bf16[2,1,1,1,1,64,512]{6,5,0,4,3,2,1:T(8,128)(2,1)S(1)}, u32[]{:S(2)}, u32[]{:S(2)}) %collective-permute-start.61) | collective-permute-done | bytes 131104 | tf_op jit(solution)/shard_map/ppermute | solution.py:103
  498.7 3.5 fusion.48
  510.8 3.5 collective-permute-done.80
  514.6 4.7 fusion.6
  523.5 6.3 %collective-permute-done.52 = bf16[2,1,1,1,2,64,512]{6,5,4,3,2,1,0:T(8,128)(2,1)S(1)} collective-permute-done((bf16[2,1,1,1,2,64,512]{6,5,4,3,2,1,0:T(8,128)(2,1)S(1)}, bf16[2,1,1,1,2,64,512]{6,5,4,3,2,1,0:T(8,128)(2,1)S(1)}, u32[]{:S(2)}, u32[]{:S(2)}) %collective-permute-start.52) | collective-permute-done | bytes 262176 | tf_op jit(solution)/shard_map/ppermute | solution.py:103
  533.2 3.5 collective-permute-start.49
  (697 shorter events, 268.5 us)
Async XLA Ops:
  6.4 34.8 %collective-permute-start.15 = (bf16[2,1,1,1,1,64,512]{6,5,0,4,3,2,1:T(8,128)(2,1)S(1)}, bf16[2,1,1,1,1,64,512]{6,5,0,4,3,2,1:T(8,128)(2,1)S(1)}, u32[]{:S(2)}, u32[]{:S(2)}) collective-permute-start(bf16[2,1,1,1,1,64,512]{6,5,0,4,3,2,1:T(8,128)(2,1)S(1)} %slice_bitcast_fusion.8), channel_id=1, source_target_pairs={{0,16},{2,18},{4,20},{6,22},{8,24},{10,26},{12,28},{14,30},{16,0},... | collective-permute-start | bytes 393224 | tf_op jit(solution)/shard_map/ppermute | solution.py:103
  7.4 30.8 %collective-permute-start.9 = (bf16[2,1,1,1,1,64,512]{6,5,0,4,3,2,1:T(8,128)(2,1)S(1)}, bf16[2,1,1,1,1,64,512]{6,5,0,4,3,2,1:T(8,128)(2,1)S(1)}, u32[]{:S(2)}, u32[]{:S(2)}) collective-permute-start(bf16[2,1,1,1,1,64,512]{6,5,0,4,3,2,1:T(8,128)(2,1)S(1)} %slice_bitcast_fusion.9), channel_id=1, source_target_pairs={{0,16},{2,18},{4,20},{6,22},{8,24},{10,26},{12,28},{14,30},{16,0},... | collective-permute-start | bytes 393224 | tf_op jit(solution)/shard_map/ppermute | solution.py:103
  41.2 44.3 %collective-permute-start = (bf16[256,1024]{1,0:T(8,128)(2,1)S(1)}, bf16[256,1024]{1,0:T(8,128)(2,1)S(1)}, u32[]{:S(2)}, u32[]{:S(2)}) collective-permute-start(bf16[256,1024]{1,0:T(8,128)(2,1)S(1)} %fusion.64), channel_id=1, source_target_pairs={{0,1},{1,0},{2,3},{3,2},{4,5},{5,4},{6,7},{7,6},{8,9},{9,8},{10,11... | collective-permute-start | bytes 1572872 | tf_op jit(solution)/shard_map/ppermute | solution.py:30
  44.2 32.2 %collective-permute-start.16 = (bf16[2,1,1,1,2,64,512]{6,5,0,4,3,2,1:T(8,128)(2,1)S(1)}, bf16[2,1,1,1,2,64,512]{6,5,0,4,3,2,1:T(8,128)(2,1)S(1)}, u32[]{:S(2)}, u32[]{:S(2)}) collective-permute-start(bf16[2,1,1,1,2,64,512]{6,5,0,4,3,2,1:T(8,128)(2,1)S(1)} %pad_maximum_fusion.32), channel_id=1, source_target_pairs={{0,8},{2,10},{4,12},{6,14},{8,0},{10,2},{12,4},{14,6},{16,24},{18,... | collective-permute-start | bytes 786440 | tf_op jit(solution)/shard_map/ppermute | solution.py:103
  76.4 37.4 %collective-permute-start.26 = (bf16[1,1,1,2,2,64,1024]{6,5,4,3,2,1,0:T(8,128)(2,1)S(1)}, bf16[1,1,1,2,2,64,1024]{6,5,4,3,2,1,0:T(8,128)(2,1)S(1)}, u32[]{:S(2)}, u32[]{:S(2)}) collective-permute-start(bf16[1,1,1,2,2,64,1024]{6,5,4,3,2,1,0:T(8,128)(2,1)S(1)} %pad_maximum_fusion.24), channel_id=1, source_target_pairs={{0,4},{2,6},{4,0},{6,2},{8,12},{10,14},{12,8},{14,10},{16,20},{18,... | collective-permute-start | bytes 1572872 | tf_op jit(solution)/shard_map/ppermute | solution.py:103
  79.1 34.2 %collective-permute-start.17 = (bf16[2,1,1,2,2,64,512]{6,5,0,4,3,2,1:T(8,128)(2,1)S(1)}, bf16[2,1,1,2,2,64,512]{6,5,0,4,3,2,1:T(8,128)(2,1)S(1)}, u32[]{:S(2)}, u32[]{:S(2)}) collective-permute-start(bf16[2,1,1,2,2,64,512]{6,5,0,4,3,2,1:T(8,128)(2,1)S(1)} %pad_maximum_fusion.22), channel_id=1, source_target_pairs={{0,4},{2,6},{4,0},{6,2},{8,12},{10,14},{12,8},{14,10},{16,20},{18,... | collective-permute-start | bytes 1572872 | tf_op jit(solution)/shard_map/ppermute | solution.py:103
  85.3 24.5 %collective-permute-start.21 = (bf16[2,1,1,2,2,64,512]{6,5,0,4,3,2,1:T(8,128)(2,1)S(1)}, bf16[2,1,1,2,2,64,512]{6,5,0,4,3,2,1:T(8,128)(2,1)S(1)}, u32[]{:S(2)}, u32[]{:S(2)}) collective-permute-start(bf16[2,1,1,2,2,64,512]{6,5,0,4,3,2,1:T(8,128)(2,1)S(1)} %pad_maximum_fusion.23), channel_id=1, source_target_pairs={{0,2},{2,0},{4,6},{6,4},{8,10},{10,8},{12,14},{14,12},{16,18},{18,... | collective-permute-start | bytes 1572872 | tf_op jit(solution)/shard_map/ppermute | solution.py:103
  106.7 47.0 %collective-permute-start.12 = (bf16[2,1,2,2,2,64,512]{6,5,0,4,3,2,1:T(8,128)(2,1)S(1)}, bf16[2,1,2,2,2,64,512]{6,5,0,4,3,2,1:T(8,128)(2,1)S(1)}, u32[]{:S(2)}, u32[]{:S(2)}) collective-permute-start(bf16[2,1,2,2,2,64,512]{6,5,0,4,3,2,1:T(8,128)(2,1)S(1)} %pad_maximum_fusion.13), channel_id=1, source_target_pairs={{0,2},{2,0},{4,6},{6,4},{8,10},{10,8},{12,14},{14,12},{16,18},{18,... | collective-permute-start | bytes 3145736 | tf_op jit(solution)/shard_map/ppermute | solution.py:103
  109.1 29.2 %collective-permute-start.30 = (bf16[1,2,2,1,1,64,1024]{6,5,4,3,2,1,0:T(8,128)(2,1)S(1)}, bf16[1,2,2,1,1,64,1024]{6,5,4,3,2,1,0:T(8,128)(2,1)S(1)}, u32[]{:S(2)}, u32[]{:S(2)}) collective-permute-start(bf16[1,2,2,1,1,64,1024]{6,5,4,3,2,1,0:T(8,128)(2,1)S(1)} %pad_maximum_fusion.25), channel_id=1, source_target_pairs={{0,16},{2,18},{4,20},{6,22},{8,24},{10,26},{12,28},{14,30},{16,0},... | collective-permute-start | bytes 1572872 | tf_op jit(solution)/shard_map/ppermute | solution.py:103
  109.9 39.5 %collective-permute-start.38 = (bf16[1,2,2,1,1,64,1024]{6,5,4,3,2,1,0:T(8,128)(2,1)S(1)}, bf16[1,2,2,1,1,64,1024]{6,5,4,3,2,1,0:T(8,128)(2,1)S(1)}, u32[]{:S(2)}, u32[]{:S(2)}) collective-permute-start(bf16[1,2,2,1,1,64,1024]{6,5,4,3,2,1,0:T(8,128)(2,1)S(1)} %pad_maximum_fusion.27), channel_id=1, source_target_pairs={{0,16},{2,18},{4,20},{6,22},{8,24},{10,26},{12,28},{14,30},{16,0},... | collective-permute-start | bytes 1572872 | tf_op jit(solution)/shard_map/ppermute | solution.py:103
  113.3 37.2 %collective-permute-start.34 = (bf16[1,1,1,2,2,64,1024]{6,5,4,3,2,1,0:T(8,128)(2,1)S(1)}, bf16[1,1,1,2,2,64,1024]{6,5,4,3,2,1,0:T(8,128)(2,1)S(1)}, u32[]{:S(2)}, u32[]{:S(2)}) collective-permute-start(bf16[1,1,1,2,2,64,1024]{6,5,4,3,2,1,0:T(8,128)(2,1)S(1)} %pad_maximum_fusion.26), channel_id=1, source_target_pairs={{0,2},{2,0},{4,6},{6,4},{8,10},{10,8},{12,14},{14,12},{16,18},{18,... | collective-permute-start | bytes 1572872 | tf_op jit(solution)/shard_map/ppermute | solution.py:103
  113.8 91.2 %collective-permute-start.14 = (bf16[128,1024]{1,0:T(8,128)(2,1)}, bf16[128,1024]{1,0:T(8,128)(2,1)S(1)}, u32[]{:S(2)}, u32[]{:S(2)}) collective-permute-start(bf16[128,1024]{1,0:T(8,128)(2,1)} %fusion.70), channel_id=1, source_target_pairs={{0,1},{1,0},{2,3},{3,2},{4,5},{5,4},{6,7},{7,6},{8,9},{9,8},{10,11... | collective-permute-start | bytes 786440 | tf_op jit(solution)/shard_map/ppermute | solution.py:30
  138.2 100.1 %collective-permute-start.27 = (bf16[1,1,2,2,2,64,1024]{6,5,4,3,2,1,0:T(8,128)(2,1)}, bf16[1,1,2,2,2,64,1024]{6,5,4,3,2,1,0:T(8,128)(2,1)}, u32[]{:S(2)}, u32[]{:S(2)}) collective-permute-start(bf16[1,1,2,2,2,64,1024]{6,5,4,3,2,1,0:T(8,128)(2,1)} %pad_maximum_fusion.16), channel_id=1, source_target_pairs={{0,2},{2,0},{4,6},{6,4},{8,10},{10,8},{12,14},{14,12},{16,18},{18,... | collective-permute-start | bytes 3145736 | tf_op jit(solution)/shard_map/ppermute | solution.py:103
  149.4 90.5 %collective-permute-start.31 = (bf16[1,2,2,1,2,64,1024]{6,5,4,3,2,1,0:T(8,128)(2,1)}, bf16[1,2,2,1,2,64,1024]{6,5,4,3,2,1,0:T(8,128)(2,1)}, u32[]{:S(2)}, u32[]{:S(2)}) collective-permute-start(bf16[1,2,2,1,2,64,1024]{6,5,4,3,2,1,0:T(8,128)(2,1)} %pad_maximum_fusion.17), channel_id=1, source_target_pairs={{0,8},{2,10},{4,12},{6,14},{8,0},{10,2},{12,4},{14,6},{16,24},{18,... | collective-permute-start | bytes 3145736 | tf_op jit(solution)/shard_map/ppermute | solution.py:103
  150.6 91.7 %collective-permute-start.39 = (bf16[1,2,2,1,2,64,1024]{6,5,4,3,2,1,0:T(8,128)(2,1)}, bf16[1,2,2,1,2,64,1024]{6,5,4,3,2,1,0:T(8,128)(2,1)}, u32[]{:S(2)}, u32[]{:S(2)}) collective-permute-start(bf16[1,2,2,1,2,64,1024]{6,5,4,3,2,1,0:T(8,128)(2,1)} %pad_maximum_fusion.19), channel_id=1, source_target_pairs={{0,8},{2,10},{4,12},{6,14},{8,0},{10,2},{12,4},{14,6},{16,24},{18,... | collective-permute-start | bytes 3145736 | tf_op jit(solution)/shard_map/ppermute | solution.py:103
  153.7 24.6 %collective-permute-start.8 = (bf16[2,2,1,2,2,64,512]{6,5,0,4,3,2,1:T(8,128)(2,1)S(1)}, bf16[2,2,1,2,2,64,512]{6,5,0,4,3,2,1:T(8,128)(2,1)S(1)}, u32[]{:S(2)}, u32[]{:S(2)}) collective-permute-start(bf16[2,2,1,2,2,64,512]{6,5,0,4,3,2,1:T(8,128)(2,1)S(1)} %pad_maximum_fusion.12), channel_id=1, source_target_pairs={{0,4},{2,6},{4,0},{6,2},{8,12},{10,14},{12,8},{14,10},{16,20},{18,... | collective-permute-start | bytes 3145736 | tf_op jit(solution)/shard_map/ppermute | solution.py:103
  286.0 26.3 %collective-permute-start.74 = (bf16[1,2,2,1,2,64,1024]{6,5,4,3,2,1,0:T(8,128)(2,1)}, bf16[1,2,2,1,2,64,1024]{6,5,4,3,2,1,0:T(8,128)(2,1)}, u32[]{:S(2)}, u32[]{:S(2)}) collective-permute-start(bf16[1,2,2,1,2,64,1024]{6,5,4,3,2,1,0:T(8,128)(2,1)} %slice.541), channel_id=1, source_target_pairs={{0,8},{2,10},{4,12},{6,14},{8,0},{10,2},{12,4},{14,6},{16,24},{18,... | collective-permute-start | bytes 3145736 | tf_op jit(solution)/shard_map/ppermute | solution.py:103
  287.0 58.3 %collective-permute-start.70 = (bf16[1,2,2,1,2,64,1024]{6,5,4,3,2,1,0:T(8,128)(2,1)}, bf16[1,2,2,1,2,64,1024]{6,5,4,3,2,1,0:T(8,128)(2,1)}, u32[]{:S(2)}, u32[]{:S(2)}) collective-permute-start(bf16[1,2,2,1,2,64,1024]{6,5,4,3,2,1,0:T(8,128)(2,1)} %slice.533), channel_id=1, source_target_pairs={{0,8},{2,10},{4,12},{6,14},{8,0},{10,2},{12,4},{14,6},{16,24},{18,... | collective-permute-start | bytes 3145736 | tf_op jit(solution)/shard_map/ppermute | solution.py:103
  294.6 53.6 %collective-permute-start.42 = (bf16[512,1024]{1,0:T(8,128)(2,1)S(1)}, bf16[512,1024]{1,0:T(8,128)(2,1)S(1)}, u32[]{:S(2)}, u32[]{:S(2)}) collective-permute-start(bf16[512,1024]{1,0:T(8,128)(2,1)S(1)} %copy-done.55), channel_id=1, source_target_pairs={{0,1},{1,0},{2,3},{3,2},{4,5},{5,4},{6,7},{7,6},{8,9},{9,8},{10,11... | collective-permute-start | bytes 3145736 | tf_op jit(solution)/shard_map/ppermute | solution.py:30
  296.5 61.1 %collective-permute-start.62 = (bf16[1,1,2,2,2,64,1024]{6,5,4,3,2,1,0:T(8,128)(2,1)S(1)}, bf16[1,1,2,2,2,64,1024]{6,5,4,3,2,1,0:T(8,128)(2,1)S(1)}, u32[]{:S(2)}, u32[]{:S(2)}) collective-permute-start(bf16[1,1,2,2,2,64,1024]{6,5,4,3,2,1,0:T(8,128)(2,1)S(1)} %slice.517), channel_id=1, source_target_pairs={{0,2},{2,0},{4,6},{6,4},{8,10},{10,8},{12,14},{14,12},{16,18},{18,... | collective-permute-start | bytes 3145736 | tf_op jit(solution)/shard_map/ppermute | solution.py:103
  296.8 67.8 %collective-permute-start.66 = (bf16[1,2,1,2,2,64,1024]{6,5,4,3,2,1,0:T(8,128)(2,1)S(1)}, bf16[1,2,1,2,2,64,1024]{6,5,4,3,2,1,0:T(8,128)(2,1)S(1)}, u32[]{:S(2)}, u32[]{:S(2)}) collective-permute-start(bf16[1,2,1,2,2,64,1024]{6,5,4,3,2,1,0:T(8,128)(2,1)S(1)} %slice.525), channel_id=1, source_target_pairs={{0,4},{2,6},{4,0},{6,2},{8,12},{10,14},{12,8},{14,10},{16,20},{18,... | collective-permute-start | bytes 3145736 | tf_op jit(solution)/shard_map/ppermute | solution.py:103
  314.9 66.1 %collective-permute-start.75 = (bf16[1,2,2,1,1,64,1024]{6,5,4,3,2,1,0:T(8,128)(2,1)}, bf16[1,2,2,1,1,64,1024]{6,5,4,3,2,1,0:T(8,128)(2,1)}, u32[]{:S(2)}, u32[]{:S(2)}) collective-permute-start(bf16[1,2,2,1,1,64,1024]{6,5,4,3,2,1,0:T(8,128)(2,1)} %slice.543), channel_id=1, source_target_pairs={{0,16},{2,18},{4,20},{6,22},{8,24},{10,26},{12,28},{14,30},{16,0},... | collective-permute-start | bytes 1572872 | tf_op jit(solution)/shard_map/ppermute | solution.py:103
  348.0 34.6 %collective-permute-start.71 = (bf16[1,2,2,1,1,64,1024]{6,5,4,3,2,1,0:T(8,128)(2,1)}, bf16[1,2,2,1,1,64,1024]{6,5,4,3,2,1,0:T(8,128)(2,1)}, u32[]{:S(2)}, u32[]{:S(2)}) collective-permute-start(bf16[1,2,2,1,1,64,1024]{6,5,4,3,2,1,0:T(8,128)(2,1)} %slice.535), channel_id=1, source_target_pairs={{0,16},{2,18},{4,20},{6,22},{8,24},{10,26},{12,28},{14,30},{16,0},... | collective-permute-start | bytes 1572872 | tf_op jit(solution)/shard_map/ppermute | solution.py:103
  358.9 25.3 %collective-permute-start.63 = (bf16[1,1,1,2,2,64,1024]{6,5,4,3,2,1,0:T(8,128)(2,1)}, bf16[1,1,1,2,2,64,1024]{6,5,4,3,2,1,0:T(8,128)(2,1)}, u32[]{:S(2)}, u32[]{:S(2)}) collective-permute-start(bf16[1,1,1,2,2,64,1024]{6,5,4,3,2,1,0:T(8,128)(2,1)} %slice.519), channel_id=1, source_target_pairs={{0,4},{2,6},{4,0},{6,2},{8,12},{10,14},{12,8},{14,10},{16,20},{18,... | collective-permute-start | bytes 1572872 | tf_op jit(solution)/shard_map/ppermute | solution.py:103
  374.8 65.6 %collective-permute-start.58 = (bf16[2,2,1,2,2,64,512]{6,5,0,4,3,2,1:T(8,128)(2,1)}, bf16[2,2,1,2,2,64,512]{6,5,0,4,3,2,1:T(8,128)(2,1)S(1)}, u32[]{:S(2)}, u32[]{:S(2)}) collective-permute-start(bf16[2,2,1,2,2,64,512]{6,5,0,4,3,2,1:T(8,128)(2,1)} %pad_maximum_fusion.8), channel_id=1, source_target_pairs={{0,4},{2,6},{4,0},{6,2},{8,12},{10,14},{12,8},{14,10},{16,20},{18,... | collective-permute-start | bytes 3145736 | tf_op jit(solution)/shard_map/ppermute | solution.py:103
  380.9 78.9 %collective-permute-start.54 = (bf16[2,1,2,2,2,64,512]{6,5,4,3,2,1,0:T(8,128)(2,1)}, bf16[2,1,2,2,2,64,512]{6,5,4,3,2,1,0:T(8,128)(2,1)S(1)}, u32[]{:S(2)}, u32[]{:S(2)}) collective-permute-start(bf16[2,1,2,2,2,64,512]{6,5,4,3,2,1,0:T(8,128)(2,1)} %pad_maximum_fusion.9), channel_id=1, source_target_pairs={{0,2},{2,0},{4,6},{6,4},{8,10},{10,8},{12,14},{14,12},{16,18},{18,... | collective-permute-start | bytes 3145736 | tf_op jit(solution)/shard_map/ppermute | solution.py:103
  382.6 60.2 %collective-permute-start.43 = (bf16[512,1024]{1,0:T(8,128)(2,1)S(1)}, bf16[512,1024]{1,0:T(8,128)(2,1)S(1)}, u32[]{:S(2)}, u32[]{:S(2)}) collective-permute-start(bf16[512,1024]{1,0:T(8,128)(2,1)S(1)} %copy-done.16), channel_id=1, source_target_pairs={{0,1},{1,0},{2,3},{3,2},{4,5},{5,4},{6,7},{7,6},{8,9},{9,8},{10,11... | collective-permute-start | bytes 3145736 | tf_op jit(solution)/shard_map/ppermute | solution.py:30
  384.2 27.5 %collective-permute-start.76 = (bf16[1,1,2,1,1,64,1024]{6,5,4,3,2,1,0:T(8,128)(2,1)S(1)}, bf16[1,1,2,1,1,64,1024]{6,5,4,3,2,1,0:T(8,128)(2,1)S(1)}, u32[]{:S(2)}, u32[]{:S(2)}) collective-permute-start(bf16[1,1,2,1,1,64,1024]{6,5,4,3,2,1,0:T(8,128)(2,1)S(1)} %slice.545), channel_id=1, source_target_pairs={{0,2},{2,0},{4,6},{6,4},{8,10},{10,8},{12,14},{14,12},{16,18},{18,... | collective-permute-start | bytes 786440 | tf_op jit(solution)/shard_map/ppermute | solution.py:103
  387.1 27.2 %collective-permute-start.72 = (bf16[1,2,1,1,1,64,1024]{6,5,4,3,2,1,0:T(8,128)(2,1)S(1)}, bf16[1,2,1,1,1,64,1024]{6,5,4,3,2,1,0:T(8,128)(2,1)S(1)}, u32[]{:S(2)}, u32[]{:S(2)}) collective-permute-start(bf16[1,2,1,1,1,64,1024]{6,5,4,3,2,1,0:T(8,128)(2,1)S(1)} %slice.537), channel_id=1, source_target_pairs={{0,4},{2,6},{4,0},{6,2},{8,12},{10,14},{12,8},{14,10},{16,20},{18,... | collective-permute-start | bytes 786440 | tf_op jit(solution)/shard_map/ppermute | solution.py:103
  441.7 29.5 %collective-permute-start.59 = (bf16[2,1,1,2,2,64,512]{6,5,0,4,3,2,1:T(8,128)(2,1)}, bf16[2,1,1,2,2,64,512]{6,5,0,4,3,2,1:T(8,128)(2,1)}, u32[]{:S(2)}, u32[]{:S(2)}) collective-permute-start(bf16[2,1,1,2,2,64,512]{6,5,0,4,3,2,1:T(8,128)(2,1)} %slice.510), channel_id=1, source_target_pairs={{0,2},{2,0},{4,6},{6,4},{8,10},{10,8},{12,14},{14,12},{16,18},{18,... | collective-permute-start | bytes 1572872 | tf_op jit(solution)/shard_map/ppermute | solution.py:103
  463.8 31.6 %collective-permute-start.50 = (bf16[2,1,2,2,2,64,512]{6,5,4,3,2,1,0:T(8,128)(2,1)S(1)}, bf16[2,1,2,2,2,64,512]{6,5,4,3,2,1,0:T(8,128)(2,1)S(1)}, u32[]{:S(2)}, u32[]{:S(2)}) collective-permute-start(bf16[2,1,2,2,2,64,512]{6,5,4,3,2,1,0:T(8,128)(2,1)S(1)} %pad_maximum_fusion.10), channel_id=1, source_target_pairs={{0,2},{2,0},{4,6},{6,4},{8,10},{10,8},{12,14},{14,12},{16,18},{18,... | collective-permute-start | bytes 3145736 | tf_op jit(solution)/shard_map/ppermute | solution.py:103
  467.9 35.9 %collective-permute-start.46 = (bf16[2,2,1,2,2,64,512]{6,5,0,4,3,2,1:T(8,128)(2,1)}, bf16[2,2,1,2,2,64,512]{6,5,0,4,3,2,1:T(8,128)(2,1)}, u32[]{:S(2)}, u32[]{:S(2)}) collective-permute-start(bf16[2,2,1,2,2,64,512]{6,5,0,4,3,2,1:T(8,128)(2,1)} %pad_maximum_fusion.11), channel_id=1, source_target_pairs={{0,4},{2,6},{4,0},{6,2},{8,12},{10,14},{12,8},{14,10},{16,20},{18,... | collective-permute-start | bytes 3145736 | tf_op jit(solution)/shard_map/ppermute | solution.py:103
  (208 other events, 2550.0 us)
